TPU v7x, 512 devices: a whole 4x4x16 slice. The times are simulated.
512 devices in a mesh: patch: 128 (over y, z, core), sub: 4 (over x).
Axes of the slice: x: 4, y: 4, z: 16, core: 2. Of those that a mesh axis runs over, the one named last changes fastest.
Arguments:
- pieces: bfloat16 [128, 4, 512, 2048], P('patch', 'sub'), may hold values from -10 to 10
- piece_slot: int32 [128, 4, 512], P('patch', 'sub'), may hold values from 0 to 1023, as said below
- piece_cell: int32 [128, 4, 512], P('patch', 'sub'), may hold values from 0 to 31
- weights: bfloat16 [128, 4, 512], P('patch', 'sub'), may hold values from 0.25 to 4
- science: bfloat16 [128, 512, 512], P('patch', 'sub'), may hold values from -12.5 to 12.5
- good_stamps: int32 [128, 32, 32], P('patch', 'sub'), may hold values 0 or 1
Outputs:
- difference: bfloat16 [128, 512, 512], P('patch', 'sub')
- coefficients: float32 [128, 19], P('patch')
Inputs may be any that keep to these rules, and one draw needn't show every extreme that they name: `piece_slot`: on each device the slots are distinct. Slot s stands for destination patch (s // 2) // 4, band (s // 2) % 4, place s % 2. In every draw one destination band, drawn from the seed, receives 2 pieces from every device.
All inputs are finite; a program needn't handle non-finite values. No bound on the sum of `good_stamps` on one device may be relied on, other than what follows from the above.
Results may differ from a plain program's by a relative error of at most 0.0094.
The roundings to bfloat16 on the way count: a program that leaves them out, or rounds other values in their place, can miss the bound.
Values may be sent and summed in bfloat16 or wider, within the bound.
A program may use at most 64 MiB of HBM per device.

v0:
```python
import math

import jax
import jax.numpy as jnp
import numpy as np
from jax import lax
from jax.sharding import PartitionSpec as P

PR = 16
PC = 128
STAMP = 16
CAP = 2
KSIZE = 23
DEGREE = 2
HALF = 11


SIGMAS = (0.75, 1.5, 3.0)
RIDGE = 0.1
BASIS_PAIRS = ((0, 0), (1, 0), (0, 1), (2, 0), (1, 1), (0, 2))


def padded_2(block, sides, width):
    for axis, dim in sides:
        count = lax.axis_size(axis)
        forward = [(i, i + 1) for i in range(count - 1)]
        backward = [(target, source) for source, target in forward]
        low = lax.ppermute(
            lax.slice_in_dim(block, block.shape[dim] - width, None, axis=dim), axis, forward
        )
        high = lax.ppermute(lax.slice_in_dim(block, 0, width, axis=dim), axis, backward)
        block = jnp.concatenate([low, block, high], axis=dim)
    return block


def filter_table():
    result = []
    for sigma in SIGMAS:
        for power in range(DEGREE + 1):
            entries = []
            for offset in range(KSIZE):
                position = float(offset - HALF)
                entries.append(
                    math.exp(-position * position / (2.0 * sigma * sigma))
                    * (position / sigma) ** power
                )
            norm_value = math.sqrt(sum([entry * entry for entry in entries]))
            result.append([entry / norm_value for entry in entries])
    return np.array(result, dtype=np.float32)


def basis_terms():
    return [(gauss, pair[0], pair[1]) for gauss in range(len(SIGMAS)) for pair in BASIS_PAIRS]


def band_matrices(length):
    filters = filter_table()
    matrix = np.zeros((filters.shape[0], length + KSIZE - 1, length), np.float32)
    positions = np.arange(length)
    for shift in range(KSIZE):
        matrix[:, positions + shift, positions] = filters[:, shift][:, None]
    return jnp.asarray(matrix).astype(jnp.bfloat16)


def shards(pieces, piece_slot, piece_cell, weights, science, good_stamps):
    n_patch = lax.axis_size("patch")
    n_sub = lax.axis_size("sub")
    total_slots = n_patch * n_sub * CAP
    features = pieces.shape[-1]
    band_rows = science.shape[1]
    width = science.shape[2]
    flat_pieces = pieces.reshape(-1, features)
    slot_index = piece_slot.reshape(-1)
    labels = jnp.stack([weights.reshape(-1), piece_cell.reshape(-1).astype(jnp.bfloat16)], axis=1)
    outgoing = jnp.zeros((total_slots, features), jnp.bfloat16).at[slot_index].set(flat_pieces)
    outgoing = outgoing.reshape(n_patch, n_sub, CAP, features)
    out_labels = jnp.zeros((total_slots, 2), jnp.bfloat16).at[slot_index].set(labels)
    out_labels = out_labels.reshape(n_patch, n_sub, CAP, 2)
    incoming, in_labels = (
        lax.all_to_all(
            lax.all_to_all(outgoing, "patch", split_axis=0, concat_axis=0, tiled=True),
            "sub",
            split_axis=1,
            concat_axis=1,
            tiled=True,
        ),
        lax.all_to_all(
            lax.all_to_all(out_labels, "patch", split_axis=0, concat_axis=0, tiled=True),
            "sub",
            split_axis=1,
            concat_axis=1,
            tiled=True,
        ),
    )
    incoming = incoming.reshape(total_slots, features)
    in_labels = in_labels.reshape(total_slots, 2)
    in_weight = in_labels[:, 0]
    in_cell = in_labels[:, 1].astype(jnp.int32)
    cell_rows = band_rows // PR
    cell_cols = width // PC
    cell_count = cell_rows * cell_cols
    placing = jnp.where(
        in_cell[None, :] == jnp.arange(cell_count, dtype=jnp.int32)[:, None],
        in_weight[None, :],
        jnp.zeros((), jnp.bfloat16),
    )
    numer = jnp.dot(placing, incoming, preferred_element_type=jnp.float32)
    weight_sum = jnp.sum(placing.astype(jnp.float32), axis=1)
    template = (numer / jnp.maximum(weight_sum, 1.0)[:, None]).astype(jnp.bfloat16)
    template = (
        template.reshape(cell_rows, cell_cols, PR, PC)
        .transpose(0, 2, 1, 3)
        .reshape(band_rows, width)
    )
    padded = padded_2(template, (("sub", 0),), HALF)
    row_block = min(band_rows, 128)
    vertical_band = band_matrices(row_block)
    window = padded
    vertical_parts = jnp.einsum(
        "fab,ax->fbx", vertical_band, window, preferred_element_type=jnp.float32
    ).astype(jnp.bfloat16)
    col_block = min(width, 128)
    horizontal_band = band_matrices(col_block)
    terms = basis_terms()
    source_index = np.array(
        [gauss * (DEGREE + 1) + power_v for gauss, power_h, power_v in terms], np.int32
    )
    filter_index = np.array(
        [gauss * (DEGREE + 1) + power_h for gauss, power_h, power_v in terms], np.int32
    )
    chosen_band = horizontal_band[filter_index]
    widened = jnp.pad(vertical_parts, ((0, 0), (0, 0), (HALF, HALF)))
    basis_parts = []
    for col_start in range(0, width, col_block):
        window = widened[:, :, col_start : col_start + col_block + 2 * HALF][source_index]
        basis_parts.append(
            jnp.einsum(
                "kra,kab->krb", window, chosen_band, preferred_element_type=jnp.float32
            ).astype(jnp.bfloat16)
        )
    basis = jnp.concatenate(basis_parts, axis=2)
    stamp_rows = good_stamps.shape[1]
    stamp_cols = good_stamps.shape[2]
    mask = jnp.broadcast_to(
        (good_stamps[0] == 1)[:, None, :, None], (stamp_rows, STAMP, stamp_cols, STAMP)
    ).reshape(band_rows, width)
    science_img = science[0]
    masked_basis = jnp.where(mask[None], basis, jnp.zeros((), jnp.bfloat16))
    cross = jnp.einsum("krw,lrw->kl", masked_basis, basis, preferred_element_type=jnp.float32)
    basis_sums = jnp.sum(masked_basis, axis=(1, 2), dtype=jnp.float32)
    basis_science = jnp.einsum(
        "krw,rw->k", masked_basis, science_img, preferred_element_type=jnp.float32
    )
    good_count = jnp.sum(mask.astype(jnp.float32))
    science_sum = jnp.sum(jnp.where(mask, science_img.astype(jnp.float32), jnp.float32(0.0)))
    upper_rows = jnp.concatenate([cross, basis_sums[:, None]], axis=1)
    lower_row = jnp.concatenate([basis_sums, good_count[None]])[None, :]
    normal_part = jnp.concatenate([upper_rows, lower_row], axis=0)
    rhs_part = jnp.concatenate([basis_science, science_sum[None]])
    unknowns = normal_part.shape[0]
    normal, rhs = lax.psum((normal_part, rhs_part), "sub")
    normal = normal + RIDGE * jnp.diag(jnp.diag(normal))
    factor = jnp.linalg.cholesky(normal)
    middle = lax.linalg.triangular_solve(factor, rhs[:, None], left_side=True, lower=True)
    solution = lax.linalg.triangular_solve(
        factor, middle, left_side=True, lower=True, transpose_a=True
    )[:, 0]
    model = jnp.zeros((band_rows, width), jnp.float32) + solution[unknowns - 1]
    for index in range(unknowns - 1):
        model = model + solution[index] * basis[index].astype(jnp.float32)
    difference = jnp.where(mask, science_img.astype(jnp.float32) - model, jnp.float32(0.0)).astype(
        jnp.bfloat16
    )
    return (difference[None], solution[None])


def solution(mesh):
    in_specs = (
        P("patch", "sub", None, None),
        P("patch", "sub", None),
        P("patch", "sub", None),
        P("patch", "sub", None),
        P("patch", "sub", None),
        P("patch", "sub", None),
    )
    out_specs = (P("patch", "sub", None), P("patch", None))
    return jax.shard_map(shards, mesh=mesh, in_specs=in_specs, out_specs=out_specs, check_vma=False)
```

profile of v0, /device:TPU:40, one launch (start us, length us, event | category | flops | bytes accessed | tf_op | source)
XLA Modules:
  0.0 417.4 jit_solution(15430124722674052)
XLA Ops:
  0.6 0.8 compare_select_fusion
  1.5 0.7 convert_bitcast_fusion
  2.2 0.7 pad_maximum_fusion.2
  2.9 0.2 copy.86
  3.0 1.8 scatter_custom_fusion
  4.9 2.3 copy.88
  7.1 19.2 %all-to-all-start = ((bf16[128,4,2,2]{1,3,2,0:T(2,128)(2,1)}), bf16[128,4,2,2]{1,3,2,0:T(2,128)(2,1)S(1)}, u32[]{:S(2)}, u32[]{:S(2)}) async-start(bf16[128,4,2,2]{1,3,2,0:T(2,128)(2,1)} %copy.88), calls=%async_computation | async-start | bytes 262144 | tf_op jit(solution)/shard_map/all_to_all | solution.py:88
  26.3 6.2 %scatter_custom_fusion.1 = bf16[1024,2048]{1,0:T(8,128)(2,1)} fusion(s32[512]{0:T(512)S(1)} %bitcast.114, bf16[1,1,512,2048]{3,2,1,0:T(8,128)(2,1)S(1)} %copy-done, bf16[]{:T(256)} %constant.71.clone.1), kind=kCustom, calls=%fused_computation.12 | custom fusion | bytes 6291458 | tf_op jit(solution)/shard_map/scatter | solution.py:75
  32.5 7.7 %reshape.122 = bf16[128,4,2,2048]{3,2,1,0:T(2,128)(2,1)} reshape(bf16[1024,2048]{1,0:T(8,128)(2,1)} %scatter_custom_fusion.1) | data formatting | bytes 8388608 | tf_op jit(solution)/shard_map/reshape | solution.py:76
  40.2 2.6 all-to-all-done
  42.8 14.1 %all-to-all-start.2 = ((bf16[128,4,2,2048]{3,2,1,0:T(2,128)(2,1)}), bf16[128,4,2,2048]{3,2,1,0:T(2,128)(2,1)}, u32[]{:S(2)}, u32[]{:S(2)}) async-start(bf16[128,4,2,2048]{3,2,1,0:T(2,128)(2,1)} %reshape.122), calls=%async_computation.2 | async-start | bytes 8388608 | tf_op jit(solution)/shard_map/all_to_all | solution.py:81
  56.8 0.7 copy.89
  57.5 188.3 %all-to-all-done.2 = bf16[128,4,2,2048]{3,2,1,0:T(2,128)(2,1)} async-done(((bf16[128,4,2,2048]{3,2,1,0:T(2,128)(2,1)}), bf16[128,4,2,2048]{3,2,1,0:T(2,128)(2,1)}, u32[]{:S(2)}, u32[]{:S(2)}) %all-to-all-start.2) | async-done | bytes 4194336 | tf_op jit(solution)/shard_map/all_to_all | solution.py:81
  245.8 4.3 %all-to-all-start.1 = ((bf16[128,4,2,2]{0,3,2,1:T(2,128)(2,1)}), bf16[128,4,2,2]{0,3,2,1:T(2,128)(2,1)S(1)}, u32[]{:S(2)}, u32[]{:S(2)}) async-start(bf16[128,4,2,2]{0,3,2,1:T(2,128)(2,1)} %copy.89), calls=%async_computation.1 | async-start | bytes 8192 | tf_op jit(solution)/shard_map/all_to_all | solution.py:87
  250.1 7.4 %copy.91 = bf16[128,4,2,2048]{3,2,0,1:T(2,128)(2,1)} copy(bf16[128,4,2,2048]{3,2,1,0:T(2,128)(2,1)} %all-to-all-done.2) | data formatting | bytes 8388608 | tf_op jit(solution)/shard_map/all_to_all | solution.py:81
  257.5 5.0 %all-to-all-start.3 = ((bf16[128,4,2,2048]{3,2,0,1:T(2,128)(2,1)}), bf16[128,4,2,2048]{3,2,0,1:T(2,128)(2,1)}, u32[]{:S(2)}, u32[]{:S(2)}) async-start(bf16[128,4,2,2048]{3,2,0,1:T(2,128)(2,1)} %copy.91), calls=%async_computation.3 | async-start | bytes 8388608 | tf_op jit(solution)/shard_map/all_to_all | solution.py:80
  262.5 0.1 copy.84
  262.7 0.2 broadcast_in_dim.107
  262.9 1.8 reshape.117
  264.7 0.2 copy.100
  264.9 0.9 broadcast_reduce_fusion
  265.7 0.8 fusion.6
  266.5 0.2 copy.90
  266.7 0.3 reshape.120
  267.1 0.1 convert_reduce_fusion.1
  267.2 43.1 %all-to-all-done.3 = bf16[128,4,2,2048]{3,2,0,1:T(2,128)(2,1)} async-done(((bf16[128,4,2,2048]{3,2,0,1:T(2,128)(2,1)}), bf16[128,4,2,2048]{3,2,0,1:T(2,128)(2,1)}, u32[]{:S(2)}, u32[]{:S(2)}) %all-to-all-start.3) | async-done | bytes 4194336 | tf_op jit(solution)/shard_map/all_to_all | solution.py:80
  310.3 9.3 %copy.92 = bf16[128,4,2,2048]{3,2,1,0:T(2,128)(2,1)} copy(bf16[128,4,2,2048]{3,2,0,1:T(2,128)(2,1)} %all-to-all-done.3) | data formatting | bytes 8388608 | tf_op jit(solution)/shard_map/all_to_all | solution.py:80
  319.6 7.2 %reshape.123 = bf16[1024,2048]{1,0:T(8,128)(2,1)} reshape(bf16[128,4,2,2048]{3,2,1,0:T(2,128)(2,1)} %copy.92) | data formatting | bytes 8388608 | tf_op jit(solution)/shard_map/reshape | solution.py:95
  326.8 3.1 fusion.5
  330.0 2.5 collective-permute-start
  332.4 1.5 collective-permute-start.1
  334.0 1.8 broadcast_in_dim.108
  335.7 0.8 copy.85
  336.5 1.6 collective-permute-done.1
  338.1 0.6 fusion.4
  338.6 1.3 pad_slice_fusion.1
  339.9 2.6 gather_fusion
  342.6 2.5 gather_fusion.3
  345.1 2.5 convolution_convert_fusion.4
  347.6 2.5 convolution_convert_fusion.1
  350.0 1.6 gather_fusion.2
  351.6 2.5 convolution_convert_fusion.2
  354.0 1.6 gather_fusion.1
  355.6 1.8 convolution_convert_fusion.3
  357.3 3.1 pad_maximum_fusion
  360.5 2.1 convert_reduce_fusion
  362.6 0.7 maximum_bitcast_fusion.2
  363.3 0.1 copy.97
  363.4 4.8 %copy.94 = bf16[18,128,512]{2,0,1:T(8,128)(2,1)} copy(bf16[18,128,512]{1,2,0:T(8,128)(2,1)} %get-tuple-element.17) | data formatting | bytes 4718592 | tf_op jit(solution)/shard_map/jit(_where)/select_n | solution.py:148
  368.2 4.8 %copy.95 = bf16[18,128,512]{2,0,1:T(8,128)(2,1)} copy(bf16[18,128,512]{1,2,0:T(8,128)(2,1)} %pad_maximum_fusion) | data formatting | bytes 4718592 | tf_op jit(solution)/shard_map/concatenate | solution.py:141
  373.0 3.1 convolution_bitcast_fusion.1
  376.1 3.1 convolution_bitcast_fusion
  379.2 0.8 pad_maximum_fusion.3
  380.0 15.9 %all-reduce.1 = (f32[19,19]{1,0:T(8,128)S(1)}, f32[19]{0:T(128)S(1)}) all-reduce(f32[19,19]{1,0:T(8,128)S(1)} %pad_maximum_fusion.1, f32[19]{0:T(128)S(1)} %pad_maximum_fusion.3), channel_id=1, replica_groups=mesh['patch'=128,'sub'=4] {'sub'}, use_global_device_ids=true, to_apply=%region_5.6 | all-reduce | flops 380 | bytes 3040 | tf_op jit(solution)/shard_map/psum | solution.py:161
  395.9 0.8 gather_fusion.4
  397.0 1.7 cholesky.16
  398.7 0.6 compare_reduce_fusion
  399.4 0.6 fusion.21
  400.0 1.5 custom-call.8
  401.5 0.1 convolution_bitcast_fusion.2
  401.6 0.1 fusion.22
  401.8 0.7 fusion.31
  402.5 14.1 %fusion.8 = bf16[1,128,512]{1,2,0:T(8,128)(2,1)S(1)} fusion(pred[1,128,512]{1,2,0:T(8,128)(4,1)S(1)} %copy-done.9, bf16[1,128,512]{1,2,0:T(8,128)(2,1)S(1)} %copy-done.7, bf16[18,128,512]{1,2,0:T(8,128)(2,1)} %pad_maximum_fusion, f32[]{:T(128)} %bitcast.45, f32[]{:T(128)} %bitcast.44, f32[]{:T(128)} %bitcast.43, f32[]{:T(128)} %bitcast.42, f32[]{:T(128)} %bitcast.41, ...), kind=kLoop, calls=%fused_computation.32 | loop fusion | flops 3801088 | bytes 2687052 | tf_op jit(solution)/shard_map/convert_element_type | solution.py:171
  416.6 0.8 copy.101
  (50 shorter events, 0.6 us)
Async XLA Ops:
  0.6 25.7 %copy-start = (bf16[1,1,512,2048]{3,2,1,0:T(8,128)(2,1)S(1)}, bf16[1,1,512,2048]{3,2,1,0:T(8,128)(2,1)}, u32[]{:S(2)}) copy-start(bf16[1,1,512,2048]{3,2,1,0:T(8,128)(2,1)} %param.15) | copy-start | bytes 6291460
  7.1 35.6 %all-to-all-start = ((bf16[128,4,2,2]{1,3,2,0:T(2,128)(2,1)}), bf16[128,4,2,2]{1,3,2,0:T(2,128)(2,1)S(1)}, u32[]{:S(2)}, u32[]{:S(2)}) async-start(bf16[128,4,2,2]{1,3,2,0:T(2,128)(2,1)} %copy.88), calls=%async_computation | async-start | bytes 262144 | tf_op jit(solution)/shard_map/all_to_all | solution.py:88
  42.8 203.1 %all-to-all-start.2 = ((bf16[128,4,2,2048]{3,2,1,0:T(2,128)(2,1)}), bf16[128,4,2,2048]{3,2,1,0:T(2,128)(2,1)}, u32[]{:S(2)}, u32[]{:S(2)}) async-start(bf16[128,4,2,2048]{3,2,1,0:T(2,128)(2,1)} %reshape.122), calls=%async_computation.2 | async-start | bytes 8388608 | tf_op jit(solution)/shard_map/all_to_all | solution.py:81
  245.8 11.7 %all-to-all-start.1 = ((bf16[128,4,2,2]{0,3,2,1:T(2,128)(2,1)}), bf16[128,4,2,2]{0,3,2,1:T(2,128)(2,1)S(1)}, u32[]{:S(2)}, u32[]{:S(2)}) async-start(bf16[128,4,2,2]{0,3,2,1:T(2,128)(2,1)} %copy.89), calls=%async_computation.1 | async-start | bytes 8192 | tf_op jit(solution)/shard_map/all_to_all | solution.py:87
  257.5 5.0 %copy-start.13 = (bf16[1,128,512]{2,1,0:T(8,128)(2,1)S(1)}, bf16[1,128,512]{2,1,0:T(8,128)(2,1)}, u32[]{:S(2)}) copy-start(bf16[1,128,512]{2,1,0:T(8,128)(2,1)} %param.19) | copy-start | bytes 393220
  257.5 5.1 %copy-start.15 = (s32[1,8,32]{2,1,0:T(8,128)S(1)}, s32[1,8,32]{2,1,0:T(8,128)}, u32[]{:S(2)}) copy-start(s32[1,8,32]{2,1,0:T(8,128)} %param.20) | copy-start | bytes 3076
  257.5 7.3 %copy-start.16 = (s32[18]{0:T(128)S(1)}, s32[18]{0:T(128)}, u32[]{:S(2)}) copy-start(s32[18]{0:T(128)} %constant.110) | copy-start | bytes 220
  257.5 52.7 %all-to-all-start.3 = ((bf16[128,4,2,2048]{3,2,0,1:T(2,128)(2,1)}), bf16[128,4,2,2048]{3,2,0,1:T(2,128)(2,1)}, u32[]{:S(2)}, u32[]{:S(2)}) async-start(bf16[128,4,2,2048]{3,2,0,1:T(2,128)(2,1)} %copy.91), calls=%async_computation.3 | async-start | bytes 8388608 | tf_op jit(solution)/shard_map/all_to_all | solution.py:80
  262.7 56.9 %copy-start.6 = (bf16[1,128,512]{1,2,0:T(8,128)(2,1)}, bf16[1,128,512]{1,2,0:T(8,128)(2,1)S(1)}, u32[]{:S(2)}) copy-start(bf16[1,128,512]{1,2,0:T(8,128)(2,1)S(1)} %copy.84) | copy-start | bytes 393220
  264.8 0.9 copy-start.8
  326.8 11.3 %copy-start.10 = (bf16[9,150,128]{2,1,0:T(8,128)(2,1)S(1)}, bf16[9,150,128]{2,1,0:T(8,128)(2,1)}, u32[]{:S(2)}) copy-start(bf16[9,150,128]{2,1,0:T(8,128)(2,1)} %constant.93) | copy-start | bytes 1036804
  330.0 6.6 %collective-permute-start = (bf16[11,512]{1,0:T(8,128)(2,1)S(1)}, bf16[11,512]{1,0:T(8,128)(2,1)S(1)}, u32[]{:S(2)}, u32[]{:S(2)}) collective-permute-start(bf16[11,512]{1,0:T(8,128)(2,1)S(1)} %get-tuple-element.24), channel_id=1, source_target_pairs={{0,1},{1,2},{2,3},{4,5},{5,6},{6,7},{8,9},{9,10},{10,11},{12,13},{... | collective-permute-start | bytes 33800 | tf_op jit(solution)/shard_map/ppermute | solution.py:28
  332.4 5.6 %collective-permute-start.1 = (bf16[11,512]{1,0:T(8,128)(2,1)S(1)}, bf16[11,512]{1,0:T(8,128)(2,1)S(1)}, u32[]{:S(2)}, u32[]{:S(2)}) collective-permute-start(bf16[11,512]{1,0:T(8,128)(2,1)S(1)} %get-tuple-element.25), channel_id=1, source_target_pairs={{1,0},{2,1},{3,2},{5,4},{6,5},{7,6},{9,8},{10,9},{11,10},{13,12},{... | collective-permute-start | bytes 33800 | tf_op jit(solution)/shard_map/ppermute | solution.py:31
  339.9 5.2 %copy-start.2 = (bf16[18,150,128]{2,1,0:T(8,128)(2,1)S(1)}, bf16[18,150,128]{2,1,0:T(8,128)(2,1)}, u32[]{:S(2)}) copy-start(bf16[18,150,128]{2,1,0:T(8,128)(2,1)} %constant.96) | copy-start | bytes 2073604
  355.6 4.9 %copy-start.3 = (bf16[18,128,128]{1,2,0:T(8,128)(2,1)S(1)}, bf16[18,128,128]{1,2,0:T(8,128)(2,1)}, u32[]{:S(2)}) copy-start(bf16[18,128,128]{1,2,0:T(8,128)(2,1)} %convolution_convert_fusion.4) | copy-start | bytes 1769476
  355.6 4.9 %copy-start.4 = (bf16[18,128,128]{1,2,0:T(8,128)(2,1)S(1)}, bf16[18,128,128]{1,2,0:T(8,128)(2,1)}, u32[]{:S(2)}) copy-start(bf16[18,128,128]{1,2,0:T(8,128)(2,1)} %convolution_convert_fusion.1) | copy-start | bytes 1769476
  355.6 4.9 %copy-start.5 = (bf16[18,128,128]{1,2,0:T(8,128)(2,1)S(1)}, bf16[18,128,128]{1,2,0:T(8,128)(2,1)}, u32[]{:S(2)}) copy-start(bf16[18,128,128]{1,2,0:T(8,128)(2,1)} %convolution_convert_fusion.2) | copy-start | bytes 1769476
  355.6 4.9 %copy-start.11 = (pred[128,512]{0,1:T(8,128)(4,1)S(1)}, pred[128,512]{0,1:T(8,128)(4,1)}, u32[]{:S(2)}) copy-start(pred[128,512]{0,1:T(8,128)(4,1)} %copy.85) | copy-start | bytes 196612
  368.2 4.8 %copy-start.14 = (bf16[1,128,512]{2,1,0:T(8,128)(2,1)S(1)}, bf16[1,128,512]{2,1,0:T(8,128)(2,1)}, u32[]{:S(2)}) copy-start(bf16[1,128,512]{2,1,0:T(8,128)(2,1)} %param.19) | copy-start | bytes 393220
  373.0 3.1 copy-start.1
  376.0 26.5 %copy-start.7 = (bf16[1,128,512]{1,2,0:T(8,128)(2,1)S(1)}, bf16[1,128,512]{1,2,0:T(8,128)(2,1)}, u32[]{:S(2)}) copy-start(bf16[1,128,512]{1,2,0:T(8,128)(2,1)} %copy-done.6) | copy-start | bytes 393220
  376.0 26.5 %copy-start.9 = (pred[1,128,512]{1,2,0:T(8,128)(4,1)S(1)}, pred[1,128,512]{1,2,0:T(8,128)(4,1)}, u32[]{:S(2)}) copy-start(pred[1,128,512]{1,2,0:T(8,128)(4,1)} %copy-done.8) | copy-start | bytes 196612
  401.8 15.6 %copy-start.12 = (f32[1,19]{1,0:T(1,128)}, f32[1,19]{1,0:T(1,128)S(1)}, u32[]{:S(2)}) copy-start(f32[1,19]{1,0:T(1,128)S(1)} %fusion.22) | copy-start | bytes 232
where the time goes:
time: 419 us; the launch traced here: 417 us
  waiting for transfers between devices  235 us (56%)
  local copies, waits for them, and re-layouts  69.8 us (17%)
  starting transfers between devices  46.5 us (11%)
  other arithmetic  29.5 us (7%)
  matrix products  19.2 us (5%)
  blocking collectives  15.9 us (4%)
    all_to_all x1, waiting for transfers between devices, shards(): lax.all_to_all(outgoing, 'patch', split_axis=0, concat_axis=0, tiled=True)  188 us
    all_to_all x1, waiting for transfers between devices, shards(): lax.all_to_all(lax.all_to_all(outgoing, 'patch', split_axis=0, concat_axi...  43.1 us
    all_to_all x1, starting transfers between devices, shards(): lax.all_to_all(out_labels, 'patch', split_axis=0, concat_axis=0, tiled=True)  19.2 us
    psum x1, blocking collectives, shards(): normal, rhs = lax.psum((normal_part, rhs_part), 'sub')  15.9 us
    all_to_all x1, starting transfers between devices, shards(): lax.all_to_all(outgoing, 'patch', split_axis=0, concat_axis=0, tiled=True)  14.1 us
    convert_element_type x1, other arithmetic, shards(): jnp.where(mask, science_img.astype(jnp.float32) - model, jnp.float32(0.0))  14.1 us
    all_to_all x1, local copies, waits for them, and re-layouts, shards(): lax.all_to_all(lax.all_to_all(outgoing, 'patch', split_axis=0, concat_axi...  9.32 us
    dot_general x4, matrix products, shards(): jnp.einsum('kra,kab->krb', window, chosen_band, preferred_element_type=jn...  9.14 us
  transfers between devices with their start and end apart: 6, of which 4 were waited for; matrix products, arithmetic and copies ran while one was open for 7% of the time, Pallas kernels for 0%

commit v1 on v0

v1 whole, which is shorter than its diff:
```python
import functools
import math

import jax
import jax.numpy as jnp
import numpy as np
from jax import lax
from jax.experimental import pallas as pl
from jax.experimental.pallas import tpu as pltpu
from jax.sharding import PartitionSpec as P

MESH = pl.DeviceIdType.MESH
F32 = jnp.float32
BF16 = jnp.bfloat16

NX, NY, NZ, NC = 4, 4, 16, 2
PEERS = NX * NY * NC
ROWS = 16
BAND = 128
WIDTH = 512
KSIZE = 23
DEGREE = 2
HALF = 11
SIGMAS = (0.75, 1.5, 3.0)
RIDGE = 0.1
BASIS_PAIRS = ((0, 0), (1, 0), (0, 1), (2, 0), (1, 1), (0, 2))
FEAT = 1024
TAIL = 128


def filter_table():
    result = []
    for sigma in SIGMAS:
        for power in range(DEGREE + 1):
            entries = []
            for offset in range(KSIZE):
                position = float(offset - HALF)
                entries.append(
                    math.exp(-position * position / (2.0 * sigma * sigma))
                    * (position / sigma) ** power
                )
            norm_value = math.sqrt(sum([entry * entry for entry in entries]))
            result.append([entry / norm_value for entry in entries])
    return np.array(result, dtype=np.float32)


def vertical_matrix():
    filters = filter_table()
    matrix = np.zeros((9, BAND, 256), np.float32)
    for row in range(BAND):
        for v in range(-HALF, HALF + 1):
            source = row + v
            if source < 0:
                column = BAND + ROWS + source
            elif source >= BAND:
                column = BAND + ROWS + source - BAND
            else:
                column = source
            matrix[:, row, column] = filters[:, v + HALF]
    return matrix.reshape(9 * BAND, 256).astype(jnp.bfloat16)


def horizontal_matrix():
    filters = filter_table()
    matrix = np.zeros((9, WIDTH, WIDTH), np.float32)
    for u in range(-HALF, HALF + 1):
        x = np.arange(max(0, -u), min(WIDTH, WIDTH - u))
        matrix[:, x + u, x] = filters[:, u + HALF][:, None]
    return matrix.astype(jnp.bfloat16)


def iota(shape, axis):
    return lax.broadcasted_iota(jnp.int32, shape, axis)


def kernel(
    slot_ref, cell_ref, weight_ref, science_ref, good_ref, pieces_hbm, vert_hbm, horiz_hbm,
    diff_ref, coef_ref,
    pieces, vert, horiz, onehot, send0, send1, recv0, recv1, place,
    part0, part1, ring0, ring1, tmpl, window, halo, vimg, design, gram_mine, gram_all,
    local_sem, a2a_send, a2a_recv, ring_send, ring_recv, halo_send, halo_recv, gram_send, gram_recv,
):
    p = lax.axis_index("patch")
    x = lax.axis_index("sub")
    c = lax.rem(p, NC)
    z = lax.rem(lax.div(p, NC), NZ)
    y = lax.div(p, NC * NZ)

    def patch_of(yy, zz, cc):
        return (yy * NZ + zz) * NC + cc

    load_pieces = pltpu.make_async_copy(pieces_hbm.at[0, 0], pieces, local_sem.at[0])
    load_vert = pltpu.make_async_copy(vert_hbm, vert, local_sem.at[1])
    load_horiz = pltpu.make_async_copy(horiz_hbm, horiz, local_sem.at[2])
    load_pieces.start()

    barrier = pltpu.get_barrier_semaphore()

    def peer(r):
        dy = lax.div(r, NC * NX)
        dc = lax.rem(lax.div(r, NX), NC)
        dx = lax.rem(r, NX)
        return (
            patch_of(lax.rem(y + dy, NY), z, lax.rem(c + dc, NC)),
            lax.rem(x + dx, NX),
        )

    up = (patch_of(y, lax.rem(z + 1, NZ), c), x)
    down = (patch_of(y, lax.rem(z + NZ - 1, NZ), c), x)

    def greet(r, carry):
        pl.semaphore_signal(barrier, inc=1, device_id=peer(r), device_id_type=MESH)
        return carry

    lax.fori_loop(1, PEERS, greet, 0)
    pl.semaphore_signal(barrier, inc=1, device_id=up, device_id_type=MESH)
    pl.semaphore_signal(barrier, inc=1, device_id=down, device_id_type=MESH)

    slots = slot_ref[0]
    cells = cell_ref[0]
    weights = weight_ref[0].astype(F32)
    marks = (lax.rem(cells, 4) * 8 + lax.div(cells, 4)).astype(F32)
    row = iota((128, 1), 0)
    peer_in = lax.div(row, ROWS)
    cc = lax.rem(c + lax.div(peer_in, NX), NC)
    xx = lax.rem(x + lax.rem(peer_in, NX), NX)
    within = lax.rem(row, ROWS)
    base = []
    for g in range(2):
        j = lax.div(within, 2) + 8 * g
        half = lax.div(j + 1, 2)
        off = jnp.where(lax.rem(j, 2) == 1, 8 - half, half - 8)
        zz = lax.rem(z + off + NZ, NZ)
        base.append(zz * 16 + cc * 8 + xx * 2 + lax.rem(within, 2))
    lane = iota((128, TAIL), 1)

    def select(dy, carry):
        yy = lax.rem(y + dy, NY)
        shifted = slots - yy * 256
        tail = jnp.zeros((128, TAIL), F32)
        for g in range(2):
            hit = shifted == base[g]
            onehot[g, dy] = jnp.where(hit, 1.0, 0.0).astype(BF16)
            w = jnp.sum(jnp.where(hit, weights, 0.0), axis=1, keepdims=True)
            m = jnp.sum(jnp.where(hit, marks, 0.0), axis=1, keepdims=True)
            tail = jnp.where(lane == 2 * g, w, jnp.where(lane == 2 * g + 1, m, tail))
        send0[pl.ds(dy * 8, 8), :, FEAT:] = tail.astype(BF16).reshape(8, ROWS, TAIL)
        return carry

    lax.fori_loop(0, NY, select, 0)
    recv0[0, :, FEAT:] = send0[0, :, FEAT:]

    load_pieces.wait()
    load_vert.start()
    load_horiz.start()

    def pack(chunk):
        g, h = chunk // 2, chunk % 2

        def body(dy, carry):
            picked = jnp.dot(
                onehot[g, dy], pieces[:, h * FEAT : (h + 1) * FEAT], preferred_element_type=F32
            )
            picked = picked.astype(BF16).reshape(8, ROWS, FEAT)
            if chunk == 0:
                send0[pl.ds(dy * 8, 8), :, :FEAT] = picked

                @pl.when(dy == 0)
                def _():
                    recv0[0, :, :FEAT] = picked[0]
            else:
                send1[chunk - 1, pl.ds(dy * 8, 8)] = picked

                @pl.when(dy == 0)
                def _():
                    recv1[chunk - 1, 0] = picked[0]
            return carry

        lax.fori_loop(0, NY, body, 0)

    def ends(chunk):
        if chunk == 0:
            return send0, recv0
        return send1.at[chunk - 1], recv1.at[chunk - 1]

    def send(chunk):
        source, target = ends(chunk)

        def body(r, carry):
            pltpu.make_async_remote_copy(
                src_ref=source.at[r],
                dst_ref=target.at[r],
                send_sem=a2a_send.at[chunk],
                recv_sem=a2a_recv.at[chunk],
                device_id=peer(r),
                device_id_type=MESH,
            ).start()
            return carry

        lax.fori_loop(1, PEERS, body, 0)

    def arrived(chunk):
        _, target = ends(chunk)
        rest = target.at[pl.ds(1, PEERS - 1)]
        pltpu.make_async_copy(rest, rest, a2a_recv.at[chunk]).wait()

    def sent(chunk):
        source, _ = ends(chunk)
        rest = source.at[pl.ds(1, PEERS - 1)]
        pltpu.make_async_copy(rest, rest, a2a_send.at[chunk]).wait()

    def placing(g):
        labels = recv0[:, :, FEAT:].reshape(PEERS * ROWS, TAIL).astype(F32)
        w = labels[:, 2 * g : 2 * g + 1]
        m = labels[:, 2 * g + 1 : 2 * g + 2]
        plane = lax.div(lax.rem(iota((PEERS * ROWS, 1), 0), ROWS), 2)
        key = m + (plane * 32).astype(F32)
        at = iota((PEERS * ROWS, 256), 1).astype(F32)
        spread = jnp.where(at == key, w, 0.0).T
        place[g] = spread.astype(BF16)
        total = jnp.sum(spread, axis=1, keepdims=True)
        part0[8 * g : 8 * g + 8, :, FEAT:] = jnp.broadcast_to(total, (256, TAIL)).reshape(8, 32, TAIL)

    def accumulate(chunk):
        g, h = chunk // 2, chunk % 2
        _, got = ends(chunk)
        into = part0 if h == 0 else part1
        for t in range(FEAT // 256):
            block = got[:, :, t * 256 : (t + 1) * 256].reshape(PEERS * ROWS, 256)
            numer = jnp.dot(place[g], block, preferred_element_type=F32)
            into[8 * g : 8 * g + 8, :, t * 256 : (t + 1) * 256] = numer.reshape(8, 32, 256)

    parts, rings = (part0, part1), (ring0, ring1)

    def hop(h, way, k):
        index = 0 if k == 0 else (2 * k - 1 if way == 0 else 2 * k)
        return pltpu.make_async_remote_copy(
            src_ref=parts[h].at[index],
            dst_ref=rings[h].at[way, k],
            send_sem=ring_send.at[h, way, k],
            recv_sem=ring_recv.at[h, way, k],
            device_id=up if way == 0 else down,
            device_id_type=MESH,
        )

    def step(h, k):
        for way in range(2):
            if k == 0:
                if way == h:
                    hop(h, way, 0).start()
                continue
            if k > 1 or way == h:
                hop(h, way, k - 1).wait_recv()
                index = 2 * k - 1 if way == 0 else 2 * k
                parts[h][index] += rings[h][way, k - 1]
            hop(h, way, k).start()

    def finish(h):
        for way in range(2):
            hop(h, way, 7).wait_recv()
        parts[h][15] += rings[h][0, 7] + rings[h][1, 7]

    pl.semaphore_wait(barrier, PEERS + 1)
    pack(0)
    send(0)
    pack(1)
    send(1)
    pack(2)
    pack(3)
    arrived(0)
    send(2)
    placing(0)
    accumulate(0)
    step(0, 0)
    step(0, 1)
    placing(1)
    arrived(1)
    send(3)
    accumulate(1)
    step(1, 0)
    step(0, 2)
    step(1, 1)
    step(0, 3)
    step(1, 2)
    arrived(2)
    accumulate(2)
    step(0, 4)
    step(1, 3)
    step(0, 5)
    arrived(3)
    accumulate(3)
    step(1, 4)
    step(0, 6)
    step(1, 5)
    step(0, 7)
    step(1, 6)
    step(1, 7)
    finish(0)

    weight_sum = jnp.maximum(part0[15, :, FEAT:], 1.0)
    for r in range(8):
        t = part0[15, :, r * 128 : (r + 1) * 128] / weight_sum
        for b in range(4):
            tmpl[b, pl.ds(r, 8, stride=16), :] = t[8 * b : 8 * b + 8]
    finish(1)
    for r in range(8):
        t = part1[15, :, r * 128 : (r + 1) * 128] / weight_sum
        for b in range(4):
            tmpl[b, pl.ds(r + 8, 8, stride=16), :] = t[8 * b : 8 * b + 8]
    for b in range(4):
        window[0:BAND, 128 * b : 128 * (b + 1)] = tmpl[b].astype(BF16)

    below = pltpu.make_async_remote_copy(
        src_ref=window.at[pl.ds(BAND - ROWS, ROWS)], dst_ref=halo.at[0],
        send_sem=halo_send.at[0], recv_sem=halo_recv.at[0],
        device_id=(p, lax.rem(x + 1, NX)), device_id_type=MESH,
    )
    above = pltpu.make_async_remote_copy(
        src_ref=window.at[pl.ds(0, ROWS)], dst_ref=halo.at[1],
        send_sem=halo_send.at[1], recv_sem=halo_recv.at[1],
        device_id=(p, lax.rem(x + NX - 1, NX)), device_id_type=MESH,
    )
    below.start()
    above.start()

    stamp_rows = jnp.where(lax.div(iota((BAND, 8), 0), 16) == iota((BAND, 8), 1), 1.0, 0.0)
    stamp_cols = jnp.where(lax.div(iota((32, WIDTH), 1), 16) == iota((32, WIDTH), 0), 1.0, 0.0)
    good = jnp.where(good_ref[0] == 1, 1.0, 0.0)
    mask = jnp.dot(jnp.dot(stamp_rows, good, preferred_element_type=F32), stamp_cols, preferred_element_type=F32)
    design[:, 18] = mask.astype(BF16).reshape(8, ROWS, WIDTH)
    design[:, 19] = (science_ref[0].astype(F32) * mask).astype(BF16).reshape(8, ROWS, WIDTH)
    window[BAND + 2 * ROWS :, :] = jnp.zeros((256 - BAND - 2 * ROWS, WIDTH), BF16)
    load_vert.wait()
    load_horiz.wait()

    below.wait_recv()
    above.wait_recv()
    window[BAND : BAND + ROWS, :] = jnp.where(x > 0, halo[0].astype(F32), 0.0).astype(BF16)
    window[BAND + ROWS : BAND + 2 * ROWS, :] = jnp.where(x < NX - 1, halo[1].astype(F32), 0.0).astype(BF16)

    for f in range(3):
        rows = slice(f * 3 * BAND, (f + 1) * 3 * BAND)
        vimg[rows] = jnp.dot(vert[rows], window[...], preferred_element_type=F32).astype(BF16)

    for g in range(3):
        for i in range(3):
            count = (3 - i) * BAND
            image = jnp.dot(
                vimg[g * 3 * BAND : g * 3 * BAND + count], horiz[g * 3 + i], preferred_element_type=F32
            )
            for j in range(3 - i):
                k = g * 6 + BASIS_PAIRS.index((i, j))
                part = image[j * BAND : (j + 1) * BAND].astype(BF16).astype(F32) * mask
                design[:, k] = part.astype(BF16).reshape(8, ROWS, WIDTH)

    def product(q, total):
        block = design[q].reshape(20 * ROWS, WIDTH)
        return total + lax.dot_general(
            block, block, (((1,), (1,)), ((), ())), preferred_element_type=F32
        )

    total = lax.fori_loop(0, 8, product, jnp.zeros((20 * ROWS, 20 * ROWS), F32))
    same = lax.rem(iota((320, 320), 0), ROWS) == lax.rem(iota((320, 320), 1), ROWS)
    total = jnp.sum(jnp.where(same, total, 0.0).reshape(20, ROWS, 320), axis=1)
    fold = jnp.where(lax.div(iota((320, 128), 0), ROWS) == iota((320, 128), 1), 1.0, 0.0)
    normal = jnp.dot(total, fold, preferred_element_type=F32, precision=lax.Precision.HIGHEST)
    normal = jnp.concatenate([normal, jnp.zeros((4, 128), F32)], axis=0)
    gram_mine[...] = normal
    gram_all[x] = normal

    shares = [
        pltpu.make_async_remote_copy(
            src_ref=gram_mine, dst_ref=gram_all.at[x],
            send_sem=gram_send.at[d - 1], recv_sem=gram_recv.at[d - 1],
            device_id=(p, lax.rem(x + d, NX)), device_id_type=MESH,
        )
        for d in range(1, NX)
    ]
    for share in shares:
        share.start()
    for share in shares:
        share.wait_recv()
    normal = gram_all[0] + gram_all[1] + gram_all[2] + gram_all[3]

    rows = iota((24, 128), 0)
    lanes = iota((24, 128), 1)
    diagonal = (rows == lanes) & (rows < 19)
    system = normal + jnp.where(diagonal, RIDGE * normal, 0.0)
    for k in range(19):
        pivot_row = system[k : k + 1] / system[k : k + 1, k : k + 1]
        column = jnp.where(rows[:, :1] == k, 0.0, system[:, k : k + 1])
        system = system - column * pivot_row
    rhs = system[:, 19:20]
    lead = jnp.sum(jnp.where(diagonal, system, 0.0), axis=1, keepdims=True)
    solved = rhs / jnp.where(rows[:, :1] < 19, lead, 1.0)
    coef_ref[...] = jnp.sum(jnp.where(diagonal, solved, 0.0), axis=0, keepdims=True)[:, :19]

    def model(q, carry):
        value = design[q, 19].astype(F32)
        for k in range(19):
            value = value - solved[k : k + 1] * design[q, k].astype(F32)
        diff_ref[0, pl.ds(q * ROWS, ROWS), :] = value.astype(BF16)
        return carry

    lax.fori_loop(0, 8, model, 0)

    for chunk in range(4):
        sent(chunk)
    for h in range(2):
        for way in range(2):
            for k in range(8):
                if k > 0 or way == h:
                    hop(h, way, k).wait_send()
    below.wait_send()
    above.wait_send()
    for share in shares:
        share.wait_send()


def shards(pieces, piece_slot, piece_cell, weights, science, good_stamps):
    vmem = pl.BlockSpec(memory_space=pltpu.VMEM)
    anywhere = pl.BlockSpec(memory_space=pl.ANY)
    dma = pltpu.SemaphoreType.DMA
    return pl.pallas_call(
        kernel,
        out_shape=(
            jax.ShapeDtypeStruct((1, BAND, WIDTH), BF16),
            jax.ShapeDtypeStruct((1, 19), F32),
        ),
        in_specs=[vmem] * 5 + [anywhere] * 3,
        out_specs=(vmem, vmem),
        scratch_shapes=[
            pltpu.VMEM((512, 2048), BF16),
            pltpu.VMEM((9 * BAND, 256), BF16),
            pltpu.VMEM((9, WIDTH, WIDTH), BF16),
            pltpu.VMEM((2, NY, 128, 512), BF16),
            pltpu.VMEM((PEERS, ROWS, FEAT + TAIL), BF16),
            pltpu.VMEM((3, PEERS, ROWS, FEAT), BF16),
            pltpu.VMEM((PEERS, ROWS, FEAT + TAIL), BF16),
            pltpu.VMEM((3, PEERS, ROWS, FEAT), BF16),
            pltpu.VMEM((2, 256, PEERS * ROWS), BF16),
            pltpu.VMEM((NZ, 32, FEAT + TAIL), F32),
            pltpu.VMEM((NZ, 32, FEAT), F32),
            pltpu.VMEM((2, 8, 32, FEAT + TAIL), F32),
            pltpu.VMEM((2, 8, 32, FEAT), F32),
            pltpu.VMEM((4, BAND, 128), F32),
            pltpu.VMEM((256, WIDTH), BF16),
            pltpu.VMEM((2, ROWS, WIDTH), BF16),
            pltpu.VMEM((9 * BAND, WIDTH), BF16),
            pltpu.VMEM((8, 20, ROWS, WIDTH), BF16),
            pltpu.VMEM((24, 128), F32),
            pltpu.VMEM((NX, 24, 128), F32),
            dma((3,)),
            dma((4,)),
            dma((4,)),
            dma((2, 2, 8)),
            dma((2, 2, 8)),
            dma((2,)),
            dma((2,)),
            dma((3,)),
            dma((3,)),
        ],
        compiler_params=pltpu.CompilerParams(
            collective_id=0, has_side_effects=True, vmem_limit_bytes=56 * 2**20
        ),
    )(
        piece_slot[0], piece_cell[0], weights[0], science, good_stamps, pieces,
        jnp.asarray(vertical_matrix()), jnp.asarray(horizontal_matrix()),
    )


def solution(mesh):
    in_specs = (
        P("patch", "sub", None, None),
        P("patch", "sub", None),
        P("patch", "sub", None),
        P("patch", "sub", None),
        P("patch", "sub", None),
        P("patch", "sub", None),
    )
    out_specs = (P("patch", "sub", None), P("patch", None))
    return jax.shard_map(shards, mesh=mesh, in_specs=in_specs, out_specs=out_specs, check_vma=False)
```

time: 419 us -> 110 us (0.26)
  the two profiles are of different devices: /device:TPU:40 before, /device:TPU:8 now
where the time goes in v1:
time: 110 us
  Pallas kernels  106 us (96%)
  local copies, waits for them, and re-layouts  2.74 us (2%)
    pallas_call x1, Pallas kernels, shards(): pl.pallas_call(kernel, out_shape=(jax.ShapeDtypeStruct((1, BAND, WIDTH),...  106 us
    unnamed x2, local copies, waits for them, and re-layouts  2.74 us

profile of v1, /device:TPU:8, one launch (start us, length us, event | category | flops | bytes accessed | tf_op | source)
XLA Modules:
  0.0 109.7 jit_solution(13335965382008210800)
XLA Ops:
  0.6 106.3 %shard_map.95 = (bf16[1,128,512]{2,1,0:T(8,128)(2,1)}, f32[1,19]{1,0:T(1,128)}) custom-call(s32[1,512]{1,0:T(1,128)} %bitcast.3, s32[1,512]{1,0:T(1,128)} %bitcast.4, bf16[1,512]{1,0:T(2,128)(2,1)} %bitcast.5, bf16[1,128,512]{2,1,0:T(8,128)(2,1)} %science_ref.1, s32[1,8,32]{2,1,0:T(8,128)} %good_ref.1, bf16[1,1,512,2048]{3,2,1,0:T(8,128)(2,1)} %pieces_hbm.1, ...), custom_call_target="tpu_custom_call" | custom-call | tf_op jit(solution)/shard_map/pallas_call | solution.py:424
  107.0 1.6 %copy.12 = bf16[1,128,512]{2,1,0:T(8,128)(2,1)} copy(bf16[1,128,512]{2,1,0:T(8,128)(2,1)} %get-tuple-element.4) | data formatting | bytes 262144
  108.5 1.2 %copy.13 = f32[1,19]{1,0:T(1,128)} copy(f32[1,19]{1,0:T(1,128)} %get-tuple-element.5) | data formatting | bytes 152

commit v2 on v1

--- a/solution.py
+++ b/solution.py
@@ -26,6 +26,8 @@
 BASIS_PAIRS = ((0, 0), (1, 0), (0, 1), (2, 0), (1, 1), (0, 2))
 FEAT = 1024
 TAIL = 128
+LIMIT = 10.0
+LEVELS = 32700.0
 
 
 def filter_table():
@@ -77,7 +79,7 @@
     slot_ref, cell_ref, weight_ref, science_ref, good_ref, pieces_hbm, vert_hbm, horiz_hbm,
     diff_ref, coef_ref,
     pieces, vert, horiz, onehot, send0, send1, recv0, recv1, place,
-    part0, part1, ring0, ring1, tmpl, window, halo, vimg, design, gram_mine, gram_all,
+    part0, part1, out0, out1, ring0, ring1, got, tmpl, window, halo, vimg, design, gram_mine, gram_all,
     local_sem, a2a_send, a2a_recv, ring_send, ring_recv, halo_send, halo_recv, gram_send, gram_recv,
 ):
     p = lax.axis_index("patch")
@@ -121,33 +123,36 @@
     weights = weight_ref[0].astype(F32)
     marks = (lax.rem(cells, 4) * 8 + lax.div(cells, 4)).astype(F32)
     row = iota((128, 1), 0)
-    peer_in = lax.div(row, ROWS)
+    peer_in = lax.rem(lax.div(row, 8), NC * NX)
     cc = lax.rem(c + lax.div(peer_in, NX), NC)
     xx = lax.rem(x + lax.rem(peer_in, NX), NX)
-    within = lax.rem(row, ROWS)
+    within = lax.rem(row, 8)
     base = []
-    for g in range(2):
-        j = lax.div(within, 2) + 8 * g
+    for chunk in range(4):
+        j = lax.div(within, 2) + 4 * chunk
         half = lax.div(j + 1, 2)
         off = jnp.where(lax.rem(j, 2) == 1, 8 - half, half - 8)
         zz = lax.rem(z + off + NZ, NZ)
         base.append(zz * 16 + cc * 8 + xx * 2 + lax.rem(within, 2))
     lane = iota((128, TAIL), 1)
 
-    def select(dy, carry):
-        yy = lax.rem(y + dy, NY)
-        shifted = slots - yy * 256
+    def both(a, b, width):
+        pair = [t.reshape(16, 8, width) for t in (a, b)]
+        return jnp.concatenate(pair, axis=1).astype(BF16)
+
+    def select(two, carry):
+        yy = lax.rem(y + 2 * two + lax.div(row, 64), NY) * 256
         tail = jnp.zeros((128, TAIL), F32)
-        for g in range(2):
-            hit = shifted == base[g]
-            onehot[g, dy] = jnp.where(hit, 1.0, 0.0).astype(BF16)
+        for chunk in range(4):
+            hit = slots == base[chunk] + yy
+            onehot[chunk, two] = jnp.where(hit, 1.0, 0.0).astype(BF16)
             w = jnp.sum(jnp.where(hit, weights, 0.0), axis=1, keepdims=True)
             m = jnp.sum(jnp.where(hit, marks, 0.0), axis=1, keepdims=True)
-            tail = jnp.where(lane == 2 * g, w, jnp.where(lane == 2 * g + 1, m, tail))
-        send0[pl.ds(dy * 8, 8), :, FEAT:] = tail.astype(BF16).reshape(8, ROWS, TAIL)
+            tail = jnp.where(lane == 2 * chunk, w, jnp.where(lane == 2 * chunk + 1, m, tail))
+        send0[pl.ds(two * 16, 16), :, FEAT:] = both(tail, tail, TAIL)
         return carry
 
-    lax.fori_loop(0, NY, select, 0)
+    lax.fori_loop(0, 2, select, 0)
     recv0[0, :, FEAT:] = send0[0, :, FEAT:]
 
     load_pieces.wait()
@@ -155,28 +160,29 @@
     load_horiz.start()
 
     def pack(chunk):
-        g, h = chunk // 2, chunk % 2
-
-        def body(dy, carry):
-            picked = jnp.dot(
-                onehot[g, dy], pieces[:, h * FEAT : (h + 1) * FEAT], preferred_element_type=F32
+        def body(two, carry):
+            a, b = (
+                jnp.dot(
+                    onehot[chunk, two], pieces[:, h * FEAT : (h + 1) * FEAT], preferred_element_type=F32
+                )
+                for h in range(2)
             )
-            picked = picked.astype(BF16).reshape(8, ROWS, FEAT)
+            picked = both(a, b, FEAT)
             if chunk == 0:
-                send0[pl.ds(dy * 8, 8), :, :FEAT] = picked
-
-                @pl.when(dy == 0)
+                send0[pl.ds(two * 16, 16), :, :FEAT] = picked
+
+                @pl.when(two == 0)
                 def _():
                     recv0[0, :, :FEAT] = picked[0]
             else:
-                send1[chunk - 1, pl.ds(dy * 8, 8)] = picked
-
-                @pl.when(dy == 0)
+                send1[chunk - 1, pl.ds(two * 16, 16)] = picked
+
+                @pl.when(two == 0)
                 def _():
                     recv1[chunk - 1, 0] = picked[0]
             return carry
 
-        lax.fori_loop(0, NY, body, 0)
+        lax.fori_loop(0, 2, body, 0)
 
     def ends(chunk):
         if chunk == 0:
@@ -209,33 +215,31 @@
         rest = source.at[pl.ds(1, PEERS - 1)]
         pltpu.make_async_copy(rest, rest, a2a_send.at[chunk]).wait()
 
-    def placing(g):
+    def placing(chunk):
         labels = recv0[:, :, FEAT:].reshape(PEERS * ROWS, TAIL).astype(F32)
-        w = labels[:, 2 * g : 2 * g + 1]
-        m = labels[:, 2 * g + 1 : 2 * g + 2]
+        w = labels[:, 2 * chunk : 2 * chunk + 1]
+        m = labels[:, 2 * chunk + 1 : 2 * chunk + 2]
         plane = lax.div(lax.rem(iota((PEERS * ROWS, 1), 0), ROWS), 2)
         key = m + (plane * 32).astype(F32)
         at = iota((PEERS * ROWS, 256), 1).astype(F32)
         spread = jnp.where(at == key, w, 0.0).T
-        place[g] = spread.astype(BF16)
-        total = jnp.sum(spread, axis=1, keepdims=True)
-        part0[8 * g : 8 * g + 8, :, FEAT:] = jnp.broadcast_to(total, (256, TAIL)).reshape(8, 32, TAIL)
+        place[chunk] = spread.astype(BF16)
+        total = jnp.sum(spread[:128], axis=1, keepdims=True)
+        part0[4 * chunk : 4 * chunk + 4, :, FEAT:] = jnp.broadcast_to(total, (128, TAIL)).reshape(4, 32, TAIL)
 
     def accumulate(chunk):
-        g, h = chunk // 2, chunk % 2
-        _, got = ends(chunk)
-        into = part0 if h == 0 else part1
+        _, landed = ends(chunk)
         for t in range(FEAT // 256):
-            block = got[:, :, t * 256 : (t + 1) * 256].reshape(PEERS * ROWS, 256)
-            numer = jnp.dot(place[g], block, preferred_element_type=F32)
-            into[8 * g : 8 * g + 8, :, t * 256 : (t + 1) * 256] = numer.reshape(8, 32, 256)
-
-    parts, rings = (part0, part1), (ring0, ring1)
+            block = landed[:, :, t * 256 : (t + 1) * 256].reshape(PEERS * ROWS, 256)
+            numer = jnp.dot(place[chunk], block, preferred_element_type=F32).reshape(2, 4, 32, 256)
+            part0[4 * chunk : 4 * chunk + 4, :, t * 256 : (t + 1) * 256] = numer[0]
+            part1[4 * chunk : 4 * chunk + 4, :, t * 256 : (t + 1) * 256] = numer[1]
+
+    parts, outs, rings = (part0, part1), (out0, out1), (ring0, ring1)
 
     def hop(h, way, k):
-        index = 0 if k == 0 else (2 * k - 1 if way == 0 else 2 * k)
         return pltpu.make_async_remote_copy(
-            src_ref=parts[h].at[index],
+            src_ref=outs[h].at[way, k],
             dst_ref=rings[h].at[way, k],
             send_sem=ring_send.at[h, way, k],
             recv_sem=ring_recv.at[h, way, k],
@@ -243,22 +247,43 @@
             device_id_type=MESH,
         )
 
-    def step(h, k):
+    def received(h, way, k):
+        hop(h, way, k).wait_recv()
+        if h == 0:
+            tail = ring0[way, k, :, FEAT:].astype(jnp.int32).astype(F32)
+            high, low = tail[:, 0:1], tail[:, 64:65]
+            got[way, k] = jnp.broadcast_to((high * 1024.0 + low) * (1.0 / 512.0), (32, TAIL))
+        unit = got[way, k][:, :1] * (LIMIT / LEVELS)
+        return rings[h][way, k, :, :FEAT].astype(jnp.int32).astype(F32) * unit
+
+    def step(k, way):
+        index = 0 if k == 0 else (2 * k - 1 if way == 0 else 2 * k)
+        for h in range(2):
+            value = parts[h][index, :, :FEAT]
+            joined = k > 1 or (k == 1 and way == 0)
+            if joined:
+                value = value + received(h, way, k - 1)
+            if h == 0:
+                weight = part0[index, :, FEAT:]
+                if joined:
+                    weight = weight + got[way, k - 1]
+                units = weight * 512.0
+                high = jnp.floor(units * (1.0 / 1024.0))
+                low = units - high * 1024.0
+                tail = jnp.where(iota((32, TAIL), 1) < 64, high, low)
+                out0[way, k, :, FEAT:] = tail.astype(jnp.int32).astype(jnp.int16)
+                per = (LEVELS / LIMIT) / jnp.maximum(weight, 0.25)[:, :1]
+            level = jnp.floor(value * per + 0.5)
+            outs[h][way, k, :, :FEAT] = level.astype(jnp.int32).astype(jnp.int16)
+            hop(h, way, k).start()
+
+    def finish(h):
+        total = parts[h][15, :, :FEAT]
         for way in range(2):
-            if k == 0:
-                if way == h:
-                    hop(h, way, 0).start()
-                continue
-            if k > 1 or way == h:
-                hop(h, way, k - 1).wait_recv()
-                index = 2 * k - 1 if way == 0 else 2 * k
-                parts[h][index] += rings[h][way, k - 1]
-            hop(h, way, k).start()
-
-    def finish(h):
-        for way in range(2):
-            hop(h, way, 7).wait_recv()
-        parts[h][15] += rings[h][0, 7] + rings[h][1, 7]
+            total = total + received(h, way, 7)
+            if h == 0:
+                part0[15, :, FEAT:] += got[way, 7]
+        parts[h][15, :, :FEAT] = total
 
     pl.semaphore_wait(barrier, PEERS + 1)
     pack(0)
@@ -272,29 +297,30 @@
     placing(0)
     accumulate(0)
     step(0, 0)
-    step(0, 1)
+    step(1, 0)
+    step(1, 1)
     placing(1)
+    placing(2)
+    placing(3)
+    step(2, 0)
     arrived(1)
     send(3)
     accumulate(1)
-    step(1, 0)
-    step(0, 2)
-    step(1, 1)
-    step(0, 3)
-    step(1, 2)
+    step(2, 1)
+    step(3, 0)
+    step(3, 1)
+    step(4, 0)
     arrived(2)
     accumulate(2)
-    step(0, 4)
-    step(1, 3)
-    step(0, 5)
+    step(4, 1)
+    step(5, 0)
+    step(5, 1)
+    step(6, 0)
     arrived(3)
     accumulate(3)
-    step(1, 4)
-    step(0, 6)
-    step(1, 5)
-    step(0, 7)
-    step(1, 6)
-    step(1, 7)
+    step(6, 1)
+    step(7, 0)
+    step(7, 1)
     finish(0)
 
     weight_sum = jnp.maximum(part0[15, :, FEAT:], 1.0)
@@ -409,7 +435,7 @@
     for h in range(2):
         for way in range(2):
             for k in range(8):
-                if k > 0 or way == h:
+                if k > 0 or way == 0:
                     hop(h, way, k).wait_send()
     below.wait_send()
     above.wait_send()
@@ -433,16 +459,19 @@
             pltpu.VMEM((512, 2048), BF16),
             pltpu.VMEM((9 * BAND, 256), BF16),
             pltpu.VMEM((9, WIDTH, WIDTH), BF16),
-            pltpu.VMEM((2, NY, 128, 512), BF16),
+            pltpu.VMEM((4, 2, 128, 512), BF16),
             pltpu.VMEM((PEERS, ROWS, FEAT + TAIL), BF16),
             pltpu.VMEM((3, PEERS, ROWS, FEAT), BF16),
             pltpu.VMEM((PEERS, ROWS, FEAT + TAIL), BF16),
             pltpu.VMEM((3, PEERS, ROWS, FEAT), BF16),
-            pltpu.VMEM((2, 256, PEERS * ROWS), BF16),
+            pltpu.VMEM((4, 256, PEERS * ROWS), BF16),
             pltpu.VMEM((NZ, 32, FEAT + TAIL), F32),
             pltpu.VMEM((NZ, 32, FEAT), F32),
-            pltpu.VMEM((2, 8, 32, FEAT + TAIL), F32),
-            pltpu.VMEM((2, 8, 32, FEAT), F32),
+            pltpu.VMEM((2, 8, 32, FEAT + TAIL), jnp.int16),
+            pltpu.VMEM((2, 8, 32, FEAT), jnp.int16),
+            pltpu.VMEM((2, 8, 32, FEAT + TAIL), jnp.int16),
+            pltpu.VMEM((2, 8, 32, FEAT), jnp.int16),
+            pltpu.VMEM((2, 8, 32, TAIL), F32),
             pltpu.VMEM((4, BAND, 128), F32),
             pltpu.VMEM((256, WIDTH), BF16),
             pltpu.VMEM((2, ROWS, WIDTH), BF16),

time: 110 us -> 94 us (0.85)
  Pallas kernels: 106 us -> 90.4 us
    pallas_call x1, Pallas kernels: 106 us -> 90.4 us  [shards(): pl.pallas_call(kernel, out_shape=(jax.ShapeDtypeStruct((1, BAND, WIDTH),...]
where the time goes in v2:
time: 94 us; the launch traced here: 93.8 us
  Pallas kernels  90.4 us (96%)
  local copies, waits for them, and re-layouts  2.74 us (3%)
    pallas_call x1, Pallas kernels, shards(): pl.pallas_call(kernel, out_shape=(jax.ShapeDtypeStruct((1, BAND, WIDTH),...  90.4 us
    unnamed x2, local copies, waits for them, and re-layouts  2.74 us

profile of v2, /device:TPU:8, one launch (start us, length us, event | category | flops | bytes accessed | tf_op | source)
XLA Modules:
  0.0 93.8 jit_solution(9069456274941805531)
XLA Ops:
  0.6 90.4 %shard_map.95 = (bf16[1,128,512]{2,1,0:T(8,128)(2,1)}, f32[1,19]{1,0:T(1,128)}) custom-call(s32[1,512]{1,0:T(1,128)} %bitcast.3, s32[1,512]{1,0:T(1,128)} %bitcast.4, bf16[1,512]{1,0:T(2,128)(2,1)} %bitcast.5, bf16[1,128,512]{2,1,0:T(8,128)(2,1)} %science_ref.1, s32[1,8,32]{2,1,0:T(8,128)} %good_ref.1, bf16[1,1,512,2048]{3,2,1,0:T(8,128)(2,1)} %pieces_hbm.1, ...), custom_call_target="tpu_custom_call" | custom-call | tf_op jit(solution)/shard_map/pallas_call | solution.py:450
  91.0 1.6 %copy.12 = bf16[1,128,512]{2,1,0:T(8,128)(2,1)} copy(bf16[1,128,512]{2,1,0:T(8,128)(2,1)} %get-tuple-element.4) | data formatting | bytes 262144
  92.6 1.2 %copy.13 = f32[1,19]{1,0:T(1,128)} copy(f32[1,19]{1,0:T(1,128)} %get-tuple-element.5) | data formatting | bytes 152

commit v3 on v2

--- a/solution.py
+++ b/solution.py
@@ -192,7 +192,8 @@
     def send(chunk):
         source, target = ends(chunk)
 
-        def body(r, carry):
+        def body(i, carry):
+            r = lax.rem(i * 11, PEERS)
             pltpu.make_async_remote_copy(
                 src_ref=source.at[r],
                 dst_ref=target.at[r],
@@ -285,8 +286,8 @@
                 part0[15, :, FEAT:] += got[way, 7]
         parts[h][15, :, :FEAT] = total
 
+    pack(0)
     pl.semaphore_wait(barrier, PEERS + 1)
-    pack(0)
     send(0)
     pack(1)
     send(1)
@@ -379,18 +380,34 @@
                 part = image[j * BAND : (j + 1) * BAND].astype(BF16).astype(F32) * mask
                 design[:, k] = part.astype(BF16).reshape(8, ROWS, WIDTH)
 
-    def product(q, total):
+    def product(q, sums):
         block = design[q].reshape(20 * ROWS, WIDTH)
-        return total + lax.dot_general(
-            block, block, (((1,), (1,)), ((), ())), preferred_element_type=F32
+        corner = block[16 * ROWS :]
+        return tuple(
+            total + lax.dot_general(a, b, (((1,), (1,)), ((), ())), preferred_element_type=F32)
+            for total, a, b in zip(sums, (block, corner), (block[: 16 * ROWS], corner))
         )
 
-    total = lax.fori_loop(0, 8, product, jnp.zeros((20 * ROWS, 20 * ROWS), F32))
-    same = lax.rem(iota((320, 320), 0), ROWS) == lax.rem(iota((320, 320), 1), ROWS)
-    total = jnp.sum(jnp.where(same, total, 0.0).reshape(20, ROWS, 320), axis=1)
-    fold = jnp.where(lax.div(iota((320, 128), 0), ROWS) == iota((320, 128), 1), 1.0, 0.0)
-    normal = jnp.dot(total, fold, preferred_element_type=F32, precision=lax.Precision.HIGHEST)
-    normal = jnp.concatenate([normal, jnp.zeros((4, 128), F32)], axis=0)
+    sums = lax.fori_loop(0, 8, product, (jnp.zeros((320, 256), F32), jnp.zeros((64, 64), F32)))
+
+    def folded(total, first):
+        high, wide = total.shape
+        same = lax.rem(iota(total.shape, 0), ROWS) == lax.rem(iota(total.shape, 1), ROWS)
+        total = jnp.sum(jnp.where(same, total, 0.0).reshape(high // ROWS, ROWS, wide), axis=1)
+        fold = lax.div(iota((wide, 128), 0), ROWS) + first == iota((wide, 128), 1)
+        fold = jnp.where(fold, 1.0, 0.0)
+        return jnp.dot(total, fold, preferred_element_type=F32, precision=lax.Precision.HIGHEST)
+
+    def blank(count):
+        return jnp.zeros((count, 128), F32)
+
+    left, right = folded(sums[0], 0), folded(sums[1], 16)
+    mirror = jnp.concatenate([blank(16), left[16:20], blank(108)], axis=0).T[:24]
+    normal = (
+        jnp.concatenate([left, blank(4)], axis=0)
+        + jnp.concatenate([blank(16), right, blank(4)], axis=0)
+        + mirror
+    )
     gram_mine[...] = normal
     gram_all[x] = normal
 

time: 94 us -> 89.9 us (0.956)
  the two profiles are of different devices: /device:TPU:8 before, /device:TPU:2 now
where the time goes in v3:
time: 89.9 us; the launch traced here: 89.7 us
  Pallas kernels  86.3 us (96%)
  local copies, waits for them, and re-layouts  2.74 us (3%)
    pallas_call x1, Pallas kernels, shards(): pl.pallas_call(kernel, out_shape=(jax.ShapeDtypeStruct((1, BAND, WIDTH),...  86.3 us
    unnamed x2, local copies, waits for them, and re-layouts  2.74 us

profile of v3, /device:TPU:2, one launch (start us, length us, event | category | flops | bytes accessed | tf_op | source)
XLA Modules:
  0.0 89.7 jit_solution(3651634781940457079)
XLA Ops:
  0.6 86.3 %shard_map.95 = (bf16[1,128,512]{2,1,0:T(8,128)(2,1)}, f32[1,19]{1,0:T(1,128)}) custom-call(s32[1,512]{1,0:T(1,128)} %bitcast.3, s32[1,512]{1,0:T(1,128)} %bitcast.4, bf16[1,512]{1,0:T(2,128)(2,1)} %bitcast.5, bf16[1,128,512]{2,1,0:T(8,128)(2,1)} %science_ref.1, s32[1,8,32]{2,1,0:T(8,128)} %good_ref.1, bf16[1,1,512,2048]{3,2,1,0:T(8,128)(2,1)} %pieces_hbm.1, ...), custom_call_target="tpu_custom_call" | custom-call | tf_op jit(solution)/shard_map/pallas_call | solution.py:467
  86.9 1.6 %copy.12 = bf16[1,128,512]{2,1,0:T(8,128)(2,1)} copy(bf16[1,128,512]{2,1,0:T(8,128)(2,1)} %get-tuple-element.4) | data formatting | bytes 262144
  88.5 1.2 %copy.13 = f32[1,19]{1,0:T(1,128)} copy(f32[1,19]{1,0:T(1,128)} %get-tuple-element.5) | data formatting | bytes 152

commit v4 on v3

--- a/solution.py
+++ b/solution.py
@@ -98,23 +98,19 @@
 
     barrier = pltpu.get_barrier_semaphore()
 
+    y_at = [patch_of(lax.rem(y + dy, NY), z, 0) for dy in range(NY)]
+    c_at = [lax.rem(c + dc, NC) for dc in range(NC)]
+    x_at = [lax.rem(x + dx, NX) for dx in range(NX)]
+
     def peer(r):
-        dy = lax.div(r, NC * NX)
-        dc = lax.rem(lax.div(r, NX), NC)
-        dx = lax.rem(r, NX)
-        return (
-            patch_of(lax.rem(y + dy, NY), z, lax.rem(c + dc, NC)),
-            lax.rem(x + dx, NX),
-        )
+        dy, dc, dx = r // (NC * NX), r // NX % NC, r % NX
+        return (y_at[dy] + c_at[dc], x_at[dx])
 
     up = (patch_of(y, lax.rem(z + 1, NZ), c), x)
     down = (patch_of(y, lax.rem(z + NZ - 1, NZ), c), x)
 
-    def greet(r, carry):
+    for r in range(1, PEERS):
         pl.semaphore_signal(barrier, inc=1, device_id=peer(r), device_id_type=MESH)
-        return carry
-
-    lax.fori_loop(1, PEERS, greet, 0)
     pl.semaphore_signal(barrier, inc=1, device_id=up, device_id_type=MESH)
     pl.semaphore_signal(barrier, inc=1, device_id=down, device_id_type=MESH)
 
@@ -192,8 +188,8 @@
     def send(chunk):
         source, target = ends(chunk)
 
-        def body(i, carry):
-            r = lax.rem(i * 11, PEERS)
+        for i in range(1, PEERS):
+            r = i * 11 % PEERS
             pltpu.make_async_remote_copy(
                 src_ref=source.at[r],
                 dst_ref=target.at[r],
@@ -202,9 +198,6 @@
                 device_id=peer(r),
                 device_id_type=MESH,
             ).start()
-            return carry
-
-        lax.fori_loop(1, PEERS, body, 0)
 
     def arrived(chunk):
         _, target = ends(chunk)
@@ -292,9 +285,10 @@
     pack(1)
     send(1)
     pack(2)
+    send(2)
     pack(3)
+    send(3)
     arrived(0)
-    send(2)
     placing(0)
     accumulate(0)
     step(0, 0)
@@ -305,7 +299,6 @@
     placing(3)
     step(2, 0)
     arrived(1)
-    send(3)
     accumulate(1)
     step(2, 1)
     step(3, 0)
@@ -388,7 +381,9 @@
             for total, a, b in zip(sums, (block, corner), (block[: 16 * ROWS], corner))
         )
 
-    sums = lax.fori_loop(0, 8, product, (jnp.zeros((320, 256), F32), jnp.zeros((64, 64), F32)))
+    sums = lax.fori_loop(
+        0, 8, product, (jnp.zeros((320, 256), F32), jnp.zeros((64, 64), F32)), unroll=True
+    )
 
     def folded(total, first):
         high, wide = total.shape

time: 89.9 us -> 88.7 us (0.987)
  Pallas kernels: 86.3 us -> 85.2 us
    pallas_call x1, Pallas kernels: 86.3 us -> 85.2 us  [shards(): pl.pallas_call(kernel, out_shape=(jax.ShapeDtypeStruct((1, BAND, WIDTH),...]
where the time goes in v4:
time: 88.7 us; the launch traced here: 88.5 us
  Pallas kernels  85.2 us (96%)
  local copies, waits for them, and re-layouts  2.74 us (3%)
    pallas_call x1, Pallas kernels, shards(): pl.pallas_call(kernel, out_shape=(jax.ShapeDtypeStruct((1, BAND, WIDTH),...  85.2 us
    unnamed x2, local copies, waits for them, and re-layouts  2.74 us

profile of v4, /device:TPU:2, one launch (start us, length us, event | category | flops | bytes accessed | tf_op | source)
XLA Modules:
  0.0 88.5 jit_solution(5152461446271131444)
XLA Ops:
  0.6 85.2 %shard_map.95 = (bf16[1,128,512]{2,1,0:T(8,128)(2,1)}, f32[1,19]{1,0:T(1,128)}) custom-call(s32[1,512]{1,0:T(1,128)} %bitcast.3, s32[1,512]{1,0:T(1,128)} %bitcast.4, bf16[1,512]{1,0:T(2,128)(2,1)} %bitcast.5, bf16[1,128,512]{2,1,0:T(8,128)(2,1)} %science_ref.1, s32[1,8,32]{2,1,0:T(8,128)} %good_ref.1, bf16[1,1,512,2048]{3,2,1,0:T(8,128)(2,1)} %pieces_hbm.1, ...), custom_call_target="tpu_custom_call" | custom-call | tf_op jit(solution)/shard_map/pallas_call | solution.py:462
  85.8 1.6 %copy.12 = bf16[1,128,512]{2,1,0:T(8,128)(2,1)} copy(bf16[1,128,512]{2,1,0:T(8,128)(2,1)} %get-tuple-element.4) | data formatting | bytes 262144
  87.4 1.2 %copy.13 = f32[1,19]{1,0:T(1,128)} copy(f32[1,19]{1,0:T(1,128)} %get-tuple-element.5) | data formatting | bytes 152
